TPU v7x, 32 devices: a whole 2x2x4 slice. The times are simulated.
32 devices in a mesh: row: 8 (over z, y), col: 4 (over x, core).
Axes of the slice: x: 2, y: 2, z: 4, core: 2. Of those that a mesh axis runs over, the one named last changes fastest.
Arguments:
- pairs: float32 [6400, 6400], P('row', 'col'), may hold values from -6 to 6
- one_body: float32 [80, 80], replicated, may hold values from -0.625 to 0.625
- aux: float32 [80, 80, 512], P('row', 'col'), may hold values from -1 to 1, as said below
- weights: float32 [512], replicated, may hold values from 0.3 to 3
Outputs:
- propagated: float32 [6400, 6400], P('row', 'col')
Inputs may be any that keep to these rules, and one draw needn't show every extreme that they name: aux[p, q, a] equals aux[q, p, a].
All inputs are finite; a program needn't handle non-finite values.
Results may differ from a plain program's by a relative error of at most 0.0001.
Values sent between devices are 32-bit elements; how exact they have to be, the bound alone decides.
No kernel may reach another device: no remote copies, remote signals or barrier semaphores. Data moves between devices by JAX's collectives and lax.ppermute only.
A program may use at most 192 MiB of HBM per device.

v0:
```python
import jax
import jax.numpy as jnp
from jax import lax
from jax.sharding import PartitionSpec as P

time_step = 0.15
highest = lax.Precision.HIGHEST


def shards(pairs, one_body, aux, weights):
    orbitals = one_body.shape[0]
    first_local = pairs.shape[0] // orbitals
    third_local = pairs.shape[1] // orbitals
    aux_left = lax.all_gather(aux, "col", axis=1, tiled=True)
    aux_right = lax.all_gather(aux, "row", axis=0, tiled=True)

    def derivative(field):
        result = jnp.einsum("jm,imkl->ijkl", one_body, field, precision=highest)
        result = result - jnp.einsum("ijkm,ml->ijkl", field, one_body, precision=highest)
        applied = jnp.einsum(
            "im,mjkl->ijkl",
            one_body,
            lax.all_to_all(field, "row", split_axis=1, concat_axis=0, tiled=True),
            precision=highest,
        )
        result = result + lax.all_to_all(applied, "row", split_axis=0, concat_axis=1, tiled=True)
        applied = jnp.einsum(
            "ijml,mk->ijkl",
            lax.all_to_all(field, "col", split_axis=3, concat_axis=2, tiled=True),
            one_body,
            precision=highest,
        )
        result = result - lax.all_to_all(applied, "col", split_axis=2, concat_axis=3, tiled=True)
        first_part = jnp.einsum("ila,ijkl->jka", aux_left, field, precision=highest)
        second_part = jnp.einsum("ijkl,jka->ila", field, aux_right, precision=highest)
        first_share = lax.psum_scatter(first_part, "row", scatter_dimension=0, tiled=True) * weights
        first_proj = lax.all_gather(first_share, "row", axis=0, tiled=True)
        second_share = (
            lax.psum_scatter(second_part, "col", scatter_dimension=1, tiled=True) * weights
        )
        second_proj = lax.all_gather(second_share, "col", axis=1, tiled=True)
        result = result + jnp.einsum("ila,jka->ijkl", aux_left, first_proj, precision=highest)
        result = result - jnp.einsum("ila,jka->ijkl", second_proj, aux_right, precision=highest)
        return result

    field = pairs.reshape(first_local, orbitals, third_local, orbitals)
    first = derivative(field)
    trial = field + time_step * first
    second = derivative(trial)
    field = field + time_step / 2.0 * (first + second)
    return field.reshape(pairs.shape)


def solution(mesh):
    in_specs = (P("row", "col"), P(), P("row", "col", None), P())
    out_specs = P("row", "col")
    return jax.shard_map(shards, mesh=mesh, in_specs=in_specs, out_specs=out_specs, check_vma=False)
```

profile of v0, /device:TPU:1, one launch (start us, length us, event | category | flops | bytes accessed | tf_op | source)
XLA Modules:
  0.0 1691.1 jit_solution(16916035116559299625)
XLA Ops:
  6.5 9.7 reshape.7
  16.2 14.1 copy.125
  45.2 99.1 %all-to-all-done.2 = f32[10,80,20,80]{1,2,0,3:T(8,128)} async-done(((f32[10,80,20,80]{1,2,0,3:T(8,128)}), f32[10,80,20,80]{1,2,0,3:T(8,128)}, u32[]{:S(2)}, u32[]{:S(2)}) %all-to-all-start.2) | async-done | bytes 5120032 | tf_op jit(solution)/shard_map/all_to_all | solution.py:29
  152.3 11.5 copy.172
  163.8 18.3 %fusion.45 = f32[10,80,512]{2,1,0:T(8,128)} fusion(f32[10,80,20,80]{1,3,2,0:T(8,128)} %copy.172, f32[80,20,512]{2,1,0:T(8,128)} %all-gather.11.cloned.1.call-done), kind=kOutput, calls=%fused_computation.49 | convolution fusion | flops 7864320000 | bytes 10035200 | tf_op jit(solution)/shard_map/ijkl,jka->ila/dot_general | solution.py:35
  182.5 17.1 %fusion.34 = f32[80,20,512]{2,0,1:T(8,128)S(1)} fusion(f32[10,80,20,80]{3,2,1,0:T(8,128)} %reshape.7, f32[10,80,512]{2,0,1:T(8,128)} %all-gather.7.cloned.1.call-done), kind=kOutput, calls=%fused_computation.40 | convolution fusion | flops 7864320000 | bytes 10035200 | tf_op jit(solution)/shard_map/ila,ijkl->jka/dot_general | solution.py:34
  203.6 9.0 copy.127
  212.5 10.2 all_to_all.115
  222.7 10.0 convolution_bitcast_fusion.1
  239.0 156.7 %all-to-all-done = f32[10,80,20,80]{3,2,0,1:T(8,128)} async-done(((f32[10,80,20,80]{3,2,0,1:T(8,128)}), f32[10,80,20,80]{3,2,0,1:T(8,128)}, u32[]{:S(2)}, u32[]{:S(2)}) %all-to-all-start) | async-done | bytes 5120032 | tf_op jit(solution)/shard_map/all_to_all | solution.py:23
  395.7 11.3 all-to-all-start.3
  420.1 12.0 fusion.11
  438.5 90.4 %all-to-all-done.3 = f32[10,80,80,20]{1,3,0,2:T(8,128)} async-done(((f32[10,80,80,20]{1,3,0,2:T(8,128)}), f32[10,80,80,20]{1,3,0,2:T(8,128)}, u32[]{:S(2)}, u32[]{:S(2)}) %all-to-all-start.3) | async-done | bytes 5120032 | tf_op jit(solution)/shard_map/all_to_all | solution.py:33
  534.5 10.9 fusion.62
  545.4 9.1 copy.132
  554.5 10.1 all_to_all.119
  564.7 21.6 %fusion.21 = f32[10,80,80,20]{2,1,3,0:T(8,128)} fusion(f32[80,20,512]{2,1,0:T(8,128)} %all-gather.11.cloned.1.call-done, f32[10,80,512,1]{2,0,1,3:T(8,128)} %bitcast.164), kind=kOutput, calls=%fused_computation.28 | convolution fusion | flops 7864320000 | bytes 10035200 | tf_op jit(solution)/shard_map/ila,jka->ijkl/dot_general | solution.py:43
  586.3 174.8 %all-gather.9.cloned.1.call-done = f32[80,20,512]{2,1,0:T(8,128)} async-done(((f32[10,20,512]{2,1,0:T(8,128)}), f32[80,20,512]{2,1,0:T(8,128)}) %all-gather.9.cloned.1.call-update) | async-done | bytes 3276816 | tf_op jit(solution)/shard_map/all_gather | solution.py:37
  761.1 21.7 %fusion.25 = f32[80,20,10,80]{0,3,1,2:T(8,128)} fusion(f32[80,20,512]{2,1,0:T(8,128)} %all-gather.9.cloned.1.call-done, f32[10,80,512,1]{2,0,1,3:T(8,128)S(1)} %bitcast.160), kind=kOutput, calls=%fused_computation.32 | convolution fusion | flops 7864320000 | bytes 10035200 | tf_op jit(solution)/shard_map/ila,jka->ijkl/dot_general | solution.py:42
  782.8 11.5 all-to-all-done.1
  802.8 11.4 copy.124
  814.2 31.7 %multiply_add_fusion = (f32[10,80,20,80]{1,3,2,0:T(8,128)}, f32[10,80,20,80]{1,3,2,0:T(8,128)}) fusion(f32[10,80,20,80]{1,3,2,0:T(8,128)} %copy.172, f32[10,80,80,20]{2,1,3,0:T(8,128)} %fusion.21, f32[80,20,10,80]{0,3,1,2:T(8,128)} %fusion.25, f32[10,80,20,80]{1,3,2,0:T(8,128)} %all_to_all.119, f32[10,80,20,80]{1,3,2,0:T(8,128)} %copy.124, ...), kind=kOutput, calls=%fused_computation.21 | convolution fusion | flops 1237760000 | bytes 46105600 | tf_op jit(solution)/shard_map/ijkm,ml->ijkl/dot_general | solution.py:19
  845.9 9.9 copy.155
  863.6 13.3 copy.148
  876.9 94.5 %all-to-all-done.6 = f32[10,80,20,80]{1,2,0,3:T(8,128)} async-done(((f32[10,80,20,80]{1,2,0,3:T(8,128)}), f32[10,80,20,80]{1,2,0,3:T(8,128)}, u32[]{:S(2)}, u32[]{:S(2)}) %all-to-all-start.6) | async-done | bytes 5120032 | tf_op jit(solution)/shard_map/all_to_all | solution.py:29
  976.6 18.3 %fusion.48 = f32[10,80,512]{2,1,0:T(8,128)} fusion(f32[10,80,20,80]{1,3,2,0:T(8,128)} %get-tuple-element.9, f32[80,20,512]{2,1,0:T(8,128)} %all-gather.11.cloned.1.call-done), kind=kOutput, calls=%fused_computation.50 | convolution fusion | flops 7864320000 | bytes 10035200 | tf_op jit(solution)/shard_map/ijkl,jka->ila/dot_general | solution.py:35
  995.0 19.2 %convolution_bitcast_fusion.2 = f32[80,20,512]{2,0,1:T(8,128)S(1)} fusion(f32[10,80,20,80]{1,3,2,0:T(8,128)} %get-tuple-element.9, f32[10,80,512,1]{2,0,1,3:T(8,128)S(1)} %bitcast.161), kind=kOutput, calls=%fused_computation.39 | convolution fusion | flops 7864320000 | bytes 10035200 | tf_op jit(solution)/shard_map/ila,ijkl->jka/dot_general | solution.py:34
  1018.1 8.9 copy.157
  1027.0 10.1 all_to_all.131
  1037.2 16.7 convolution_bitcast_fusion
  1053.9 13.3 copy.159
  1067.2 154.2 %all-to-all-done.4 = f32[10,80,20,80]{3,2,0,1:T(8,128)} async-done(((f32[10,80,20,80]{3,2,0,1:T(8,128)}), f32[10,80,20,80]{3,2,0,1:T(8,128)}, u32[]{:S(2)}, u32[]{:S(2)}) %all-to-all-start.4) | async-done | bytes 5120032 | tf_op jit(solution)/shard_map/all_to_all | solution.py:23
  1228.9 33.8 %reduce-scatter.7.cloned.1.call-done = f32[10,20,512]{2,1,0:T(8,128)} async-done(((f32[80,20,512]{2,1,0:T(8,128)}), f32[10,20,512]{2,1,0:T(8,128)}) %reduce-scatter.7.cloned.1.call-update) | async-done | bytes 409616 | tf_op jit(solution)/shard_map/reduce_scatter | solution.py:36
  1270.6 15.7 fusion.31
  1286.3 13.3 copy.152
  1299.6 51.2 %all-to-all-done.7 = f32[10,80,80,20]{1,3,0,2:T(8,128)} async-done(((f32[10,80,80,20]{1,3,0,2:T(8,128)}), f32[10,80,80,20]{1,3,0,2:T(8,128)}, u32[]{:S(2)}, u32[]{:S(2)}) %all-to-all-start.7) | async-done | bytes 5120032 | tf_op jit(solution)/shard_map/all_to_all | solution.py:33
  1356.4 11.0 fusion.58
  1367.4 9.2 copy.161
  1376.6 10.1 all_to_all.135
  1386.7 21.4 %fusion.17 = f32[10,80,80,20]{2,1,3,0:T(8,128)} fusion(f32[80,20,512]{2,1,0:T(8,128)} %all-gather.11.cloned.1.call-done, f32[10,80,512,1]{2,0,1,3:T(8,128)} %bitcast.163), kind=kOutput, calls=%fused_computation.24 | convolution fusion | flops 7864320000 | bytes 10035200 | tf_op jit(solution)/shard_map/ila,jka->ijkl/dot_general | solution.py:43
  1408.1 174.3 %all-gather.15.cloned.1.call-done = f32[80,20,512]{2,1,0:T(8,128)} async-done(((f32[10,20,512]{2,1,0:T(8,128)}), f32[80,20,512]{2,1,0:T(8,128)}) %all-gather.15.cloned.1.call-update) | async-done | bytes 3276816 | tf_op jit(solution)/shard_map/all_gather | solution.py:37
  1582.5 21.4 %fusion.15 = f32[80,20,10,80]{0,3,1,2:T(8,128)} fusion(f32[80,20,512]{2,1,0:T(8,128)} %all-gather.15.cloned.1.call-done, f32[10,80,512,1]{2,0,1,3:T(8,128)S(1)} %bitcast.162), kind=kOutput, calls=%fused_computation.22 | convolution fusion | flops 7864320000 | bytes 10035200 | tf_op jit(solution)/shard_map/ila,jka->ijkl/dot_general | solution.py:42
  1603.9 12.6 all-to-all-done.5
  1616.4 8.5 copy.153
  1625.0 11.4 copy.154
  1636.4 27.2 %fusion.2 = f32[10,80,20,80]{1,3,2,0:T(8,128)} fusion(f32[10,80,20,80]{1,3,2,0:T(8,128)} %copy.172, f32[10,80,20,80]{1,3,2,0:T(8,128)} %get-tuple-element.10, f32[10,80,80,20]{2,1,3,0:T(8,128)} %fusion.17, f32[80,20,10,80]{0,3,1,2:T(8,128)} %fusion.15, f32[10,80,20,80]{1,3,2,0:T(8,128)} %all_to_all.135, f32[10,80,20,80]{1,3,2,0:T(8,128)} %copy.154, ...), kind=kOutput, calls=%fused_computation.3 | convolution fusion | flops 1239040000 | bytes 46105600 | tf_op jit(solution)/shard_map/ijkm,ml->ijkl/dot_general | solution.py:19
  1663.6 10.7 copy.173
  1674.3 9.5 reshape.8
  (58 shorter events, 104.2 us)
Async XLA Ops:
  6.5 216.2 %copy-start = (f32[80,80]{1,0:T(8,128)S(1)}, f32[80,80]{1,0:T(8,128)}, u32[]{:S(2)}) copy-start(f32[80,80]{1,0:T(8,128)} %param.5) | copy-start | bytes 76804
  30.3 113.9 %all-to-all-start.2 = ((f32[10,80,20,80]{1,2,0,3:T(8,128)}), f32[10,80,20,80]{1,2,0,3:T(8,128)}, u32[]{:S(2)}, u32[]{:S(2)}) async-start(f32[10,80,20,80]{1,2,0,3:T(8,128)} %copy.125), calls=%async_computation.2 | async-start | bytes 19660800 | tf_op jit(solution)/shard_map/all_to_all | solution.py:29
  36.3 127.5 %all-gather.11.cloned.1.call-start = ((), (), s32[]{:S(2)}) async-start(), calls=%async_computation.13 | async-start | bytes 4423680 | tf_op jit(solution)/shard_map/all_gather | solution.py:15
  45.2 106.0 %copy-start.2 = (f32[10,20,512]{2,1,0:T(8,128)S(1)}, f32[10,20,512]{2,1,0:T(8,128)}, u32[]{:S(2)}) copy-start(f32[10,20,512]{2,1,0:T(8,128)} %param.6) | copy-start | bytes 1228804
  144.3 251.4 %all-to-all-start = ((f32[10,80,20,80]{3,2,0,1:T(8,128)}), f32[10,80,20,80]{3,2,0,1:T(8,128)}, u32[]{:S(2)}, u32[]{:S(2)}) async-start(f32[10,80,20,80]{3,2,0,1:T(8,128)} %copy.118), calls=%async_computation | async-start | bytes 19660800 | tf_op jit(solution)/shard_map/all_to_all | solution.py:23
  151.1 31.4 %all-gather.7.cloned.1.call-start = ((), (), s32[]{:S(2)}) async-start(), calls=%async_computation.10 | async-start | bytes 3276800 | tf_op jit(solution)/shard_map/all_gather | solution.py:14
  152.2 264.5 %all-reduce.5.cloned.1.call-start = ((), (), s32[]{:S(2)}) async-start(), calls=%async_computation.18 | async-start | bytes 3276800
  182.2 234.6 %reduce-scatter.5.cloned.1.call-start = ((), (), s32[]{:S(2)}) async-start(), calls=%async_computation.11 | async-start | bytes 4423680 | tf_op jit(solution)/shard_map/reduce_scatter | solution.py:36
  239.0 168.0 %copy-start.4 = (u32[32]{0:T(128)S(1)}, u32[32]{0:T(128)}, u32[]{:S(2)}) copy-start(u32[32]{0:T(128)} %constant.7) | copy-start | bytes 388
  395.7 133.2 %all-to-all-start.3 = ((f32[10,80,80,20]{1,3,0,2:T(8,128)}), f32[10,80,80,20]{1,3,0,2:T(8,128)}, u32[]{:S(2)}, u32[]{:S(2)}) async-start(f32[10,80,80,20]{1,3,0,2:T(8,128)} %copy.130), calls=%async_computation.3 | async-start | bytes 19660800 | tf_op jit(solution)/shard_map/all_to_all | solution.py:33
  407.0 157.6 %all-gather.13.cloned.1.call-start = ((), (), s32[]{:S(2)}) async-start(), calls=%async_computation.14 | async-start | bytes 3276800 | tf_op jit(solution)/shard_map/all_gather | solution.py:41
  408.4 8.4 copy-start.3
  528.9 265.4 %all-to-all-start.1 = ((f32[80,10,20,80]{3,2,1,0:T(8,128)}), f32[80,10,20,80]{3,2,1,0:T(8,128)}, u32[]{:S(2)}, u32[]{:S(2)}) async-start(f32[80,10,20,80]{3,2,1,0:T(8,128)} %copy.122), calls=%async_computation.1 | async-start | bytes 19660800 | tf_op jit(solution)/shard_map/all_to_all | solution.py:26
  534.0 227.1 %all-gather.9.cloned.1.call-start = ((), (), s32[]{:S(2)}) async-start(), calls=%async_computation.12 | async-start | bytes 4423680 | tf_op jit(solution)/shard_map/all_gather | solution.py:37
  564.7 196.4 %copy-start.1 = (f32[10,80,512]{2,0,1:T(8,128)S(1)}, f32[10,80,512]{2,0,1:T(8,128)}, u32[]{:S(2)}) copy-start(f32[10,80,512]{2,0,1:T(8,128)} %all-gather.7.cloned.1.call-done) | copy-start | bytes 4915204
  855.7 115.7 %all-to-all-start.6 = ((f32[10,80,20,80]{1,2,0,3:T(8,128)}), f32[10,80,20,80]{1,2,0,3:T(8,128)}, u32[]{:S(2)}, u32[]{:S(2)}) async-start(f32[10,80,20,80]{1,2,0,3:T(8,128)} %copy.155), calls=%async_computation.7 | async-start | bytes 19660800 | tf_op jit(solution)/shard_map/all_to_all | solution.py:29
  971.4 249.9 %all-to-all-start.4 = ((f32[10,80,20,80]{3,2,0,1:T(8,128)}), f32[10,80,20,80]{3,2,0,1:T(8,128)}, u32[]{:S(2)}, u32[]{:S(2)}) async-start(f32[10,80,20,80]{3,2,0,1:T(8,128)} %copy.148), calls=%async_computation.5 | async-start | bytes 19660800 | tf_op jit(solution)/shard_map/all_to_all | solution.py:23
  976.6 252.3 %all-reduce.7.cloned.1.call-start = ((), (), s32[]{:S(2)}) async-start(), calls=%async_computation.19 | async-start | bytes 3276800
  995.0 267.7 %reduce-scatter.7.cloned.1.call-start = ((), (), s32[]{:S(2)}) async-start(), calls=%async_computation.15 | async-start | bytes 4423680 | tf_op jit(solution)/shard_map/reduce_scatter | solution.py:36
  1221.4 129.4 %all-to-all-start.7 = ((f32[10,80,80,20]{1,3,0,2:T(8,128)}), f32[10,80,80,20]{1,3,0,2:T(8,128)}, u32[]{:S(2)}, u32[]{:S(2)}) async-start(f32[10,80,80,20]{1,3,0,2:T(8,128)} %copy.159), calls=%async_computation.8 | async-start | bytes 19660800 | tf_op jit(solution)/shard_map/all_to_all | solution.py:33
  1228.9 157.8 %all-gather.17.cloned.1.call-start = ((), (), s32[]{:S(2)}) async-start(), calls=%async_computation.17 | async-start | bytes 3276800 | tf_op jit(solution)/shard_map/all_gather | solution.py:41
  1350.7 265.7 %all-to-all-start.5 = ((f32[80,10,20,80]{3,2,1,0:T(8,128)}), f32[80,10,20,80]{3,2,1,0:T(8,128)}, u32[]{:S(2)}, u32[]{:S(2)}) async-start(f32[80,10,20,80]{3,2,1,0:T(8,128)} %copy.152), calls=%async_computation.6 | async-start | bytes 19660800 | tf_op jit(solution)/shard_map/all_to_all | solution.py:26
  1355.9 226.6 %all-gather.15.cloned.1.call-start = ((), (), s32[]{:S(2)}) async-start(), calls=%async_computation.16 | async-start | bytes 4423680 | tf_op jit(solution)/shard_map/all_gather | solution.py:37
Sparse Core Ops, SparseCore 0:
  39.3 71.5 all-gather.10
  153.5 26.9 all-gather.6
  182.8 44.2 all-reduce.4
  231.1 182.9 reduce-scatter.4
  420.3 40.7 all-gather.12
  536.7 224.3 all-gather.8
  995.1 44.2 all-reduce.6
  1043.5 219.1 reduce-scatter.6
  1266.1 39.9 all-gather.16
  1358.6 223.8 all-gather.14
where the time goes:
time: 1700 us; the launch traced here: 1690 us
  waiting for transfers between devices  1050 us (62%)
  matrix products  294 us (17%)
  local copies, waits for them, and re-layouts  267 us (16%)
  starting transfers between devices  55.4 us (3%)
    all_gather x2, waiting for transfers between devices, derivative(): first_proj = lax.all_gather(first_share, 'row', axis=0, tiled=True)  349 us
    all_to_all x2, waiting for transfers between devices, derivative(): lax.all_to_all(field, 'row', split_axis=1, concat_axis=0, tiled=True)  311 us
    all_to_all x2, waiting for transfers between devices, derivative(): lax.all_to_all(field, 'col', split_axis=3, concat_axis=2, tiled=True)  194 us
    all_to_all x2, waiting for transfers between devices, derivative(): lax.all_to_all(applied, 'col', split_axis=2, concat_axis=3, tiled=True)  142 us
    dot_general x2, matrix products, derivative(): jnp.einsum('ijkm,ml->ijkl', field, one_body, precision=highest)  58.9 us
    reshape x4, local copies, waits for them, and re-layouts, shards(): field = pairs.reshape(first_local, orbitals, third_local, orbitals)  43.5 us
    dot_general x2, matrix products, derivative(): jnp.einsum('ila,jka->ijkl', aux_left, first_proj, precision=highest)  43.1 us
    dot_general x2, matrix products, derivative(): jnp.einsum('ila,jka->ijkl', second_proj, aux_right, precision=highest)  43 us
  transfers between devices with their start and end apart: 18, of which 11 were waited for; matrix products, arithmetic and copies ran while one was open for 22% of the time, Pallas kernels for 0%

commit v1 on v0

v1 whole, which is shorter than its diff:
```python
import functools

import jax
import jax.numpy as jnp
from jax import lax
from jax.experimental import pallas as pl
from jax.experimental.pallas import tpu as pltpu
from jax.sharding import PartitionSpec as P

time_step = 0.15
vmem_limit = 60 * 1024 * 1024
f32, bf16 = jnp.float32, jnp.bfloat16


def halves(x):
    high = x.astype(bf16)
    return high, (x - high.astype(f32)).astype(bf16)


def dot(a, b):
    return lax.dot_general(a, b, (((1,), (0,)), ((), ())), preferred_element_type=f32)


def dot3(a, b):
    return dot(a[0], b[0]) + dot(a[0], b[1]) + dot(a[1], b[0])


def stacked(x):
    high, low = halves(x)
    return jnp.concatenate([high, high, low], axis=0)


def call(body, out_shape, scratch=(), flops=0, moved=0):
    return pl.pallas_call(
        body,
        out_shape=out_shape,
        scratch_shapes=list(scratch),
        compiler_params=pltpu.CompilerParams(vmem_limit_bytes=vmem_limit),
        cost_estimate=pl.CostEstimate(flops=flops, bytes_accessed=moved, transcendentals=0),
    )


def regroup_body(n, x_ref, crossed_ref, turned_ref):
    for i in range(x_ref.shape[0] // n):
        for k in range(x_ref.shape[1] // n):
            a, b = slice(i * n, (i + 1) * n), slice(k * n, (k + 1) * n)
            block = x_ref[a, b]
            crossed_ref[b, a] = block
            turned_ref[a, b] = block.T


def turn_body(x_ref, out_ref):
    rows = x_ref.shape[0]
    for start in range(0, rows, 128):
        stop = min(start + 128, rows)
        out_ref[:, start:stop] = x_ref[start:stop, :].T


def finish_body(n, x_ref, crossed_ref, turned_ref, out_ref):
    for i in range(x_ref.shape[0] // n):
        for k in range(x_ref.shape[1] // n):
            a, b = slice(i * n, (i + 1) * n), slice(k * n, (k + 1) * n)
            out_ref[a, b] = x_ref[a, b] + crossed_ref[b, a] + turned_ref[a, b].T


def split_body(x_ref, high_ref, low_ref):
    high_ref[...], low_ref[...] = halves(x_ref[...])


def take(ref, rows, batch):
    tiles = [ref[t, rows, : min(128, batch - 128 * t)] for t in range(ref.shape[0])]
    return jnp.concatenate(tiles, axis=1) if len(tiles) > 1 else tiles[0]


def put(ref, rows, value):
    for t in range(ref.shape[0]):
        part = value[:, 128 * t : 128 * (t + 1)]
        ref[t, rows, : part.shape[1]] = part


def project(source_ref, high_ref, low_ref, weights_ref):
    blocks, batch, width = source_ref.shape

    def step(r, total):
        rows = pl.ds(pl.multiple_of(r * width, 16), width)
        return total + dot3(halves(source_ref[r]), (high_ref[rows, :], low_ref[rows, :]))

    total = lax.fori_loop(0, blocks, step, jnp.zeros((batch, high_ref.shape[1]), f32))
    return halves((total * weights_ref[...]).T)


def major_term(n, source_ref, major_ref, out_ref):
    def step(q, carry):
        for tile in range(source_ref.shape[0]):
            at = (tile, pl.ds(q, n, stride=n), slice(None))
            out_ref[at] = dot(major_ref[...], stacked(source_ref[at]))
        return carry

    lax.fori_loop(0, n, step, 0)


def block_result(n, r, width, source_ref, term_ref, high_ref, low_ref, minor_ref, proj):
    batch = proj[0].shape[1]
    rows = pl.ds(pl.multiple_of(r * width, 16), width)
    cycle = dot3((high_ref[rows, :], low_ref[rows, :]), proj)
    minor = []
    for p in range(width // n):
        at = pl.ds(pl.multiple_of(r * width + p * n, 16), n)
        minor.append(dot(minor_ref[...], stacked(take(source_ref, at, batch))))
    return cycle + jnp.concatenate(minor, axis=0) + take(term_ref, rows, batch)


def spread(source_ref, out_ref):
    blocks, batch, width = source_ref.shape

    def step(r, carry):
        rows = pl.ds(pl.multiple_of(r * width, 16), width)
        put(out_ref, rows, source_ref[r].T)
        return carry

    lax.fori_loop(0, blocks, step, 0)


def twice_body(n, x_ref, high_ref, low_ref, weights_ref, major_ref, minor_ref, z_ref, s_ref, xp, zp):
    blocks, batch, width = x_ref.shape
    spread(x_ref, xp)
    proj = project(x_ref, high_ref, low_ref, weights_ref)
    major_term(n, xp, major_ref, zp)

    def first(r, carry):
        rows = pl.ds(pl.multiple_of(r * width, 16), width)
        result = block_result(n, r, width, xp, zp, high_ref, low_ref, minor_ref, proj)
        put(zp, rows, result)
        z_ref[r] = result.T
        return carry

    lax.fori_loop(0, blocks, first, 0)
    proj2 = project(z_ref, high_ref, low_ref, weights_ref)
    major_term(n, zp, major_ref, xp)

    def second(r, carry):
        result = block_result(n, r, width, zp, xp, high_ref, low_ref, minor_ref, proj2)
        s_ref[r] = time_step * z_ref[r] + (time_step * time_step / 2.0) * result.T
        return carry

    lax.fori_loop(0, blocks, second, 0)


def once_body(n, keep, scale, x_ref, high_ref, low_ref, weights_ref, major_ref, minor_ref, out_ref, xp, zp):
    blocks, batch, width = x_ref.shape
    spread(x_ref, xp)
    proj = project(x_ref, high_ref, low_ref, weights_ref)
    major_term(n, xp, major_ref, zp)

    def step(r, carry):
        result = block_result(n, r, width, xp, zp, high_ref, low_ref, minor_ref, proj)
        out_ref[r] = scale * result.T + (keep * x_ref[r] if keep else 0.0)
        return carry

    lax.fori_loop(0, blocks, step, 0)


def added_body(n, x_ref, z_ref, *refs):
    blocks = x_ref.shape[0]
    *rest, total = refs

    def step(r, carry):
        total[r] = x_ref[r] + (time_step * time_step) * z_ref[r]
        return carry

    lax.fori_loop(0, blocks, step, 0)
    once_body(n, 0.0, 1.0, total, *rest)


def tripled(matrix):
    high = lax.reduce_precision(matrix, 8, 7)
    low = matrix - high
    return jnp.concatenate([high, low, high], axis=1).astype(bf16)


def exchange(x, axis):
    return lax.all_to_all(x, axis, split_axis=0, concat_axis=0, tiled=True)


def shards(rows, cols, pairs, one_body, aux, weights):
    n = one_body.shape[0]
    naux = aux.shape[2]
    local_rows, local_cols = pairs.shape
    size = local_rows * local_cols

    whole = lax.all_gather(aux, "row", axis=0, tiled=True)
    whole = lax.all_gather(whole, "col", axis=1, tiled=True).reshape(n * n, naux)
    steps = n // 10 if n % 10 == 0 else 1
    tile = n * n // steps
    shape = jax.ShapeDtypeStruct((n * n, naux), bf16)
    high, low = pl.pallas_call(
        split_body,
        grid=(steps,),
        in_specs=[pl.BlockSpec((tile, naux), lambda s: (s, 0))],
        out_specs=[pl.BlockSpec((tile, naux), lambda s: (s, 0))] * 2,
        out_shape=[shape, shape],
        compiler_params=pltpu.CompilerParams(vmem_limit_bytes=vmem_limit),
        cost_estimate=pl.CostEstimate(
            flops=2 * n * n * naux, bytes_accessed=8 * n * n * naux, transcendentals=0
        ),
    )(whole)

    left = tripled(one_body)
    right = tripled(-one_body.T)
    gain = weights.reshape(1, naux)

    crossed, turned = call(
        functools.partial(regroup_body, n),
        [
            jax.ShapeDtypeStruct((local_cols, local_rows), f32),
            jax.ShapeDtypeStruct((local_rows, local_cols), f32),
        ],
        moved=12 * size,
    )(pairs)

    def operator(body, arrays, plus, major, minor, outs, extra=()):
        blocks, batch, width = arrays[0].shape
        shape = jax.ShapeDtypeStruct((blocks, batch, width), f32)
        work = pltpu.VMEM((-(-batch // 128), n * n, 128), f32)
        return call(
            functools.partial(body, n),
            [shape] * outs if outs > 1 else shape,
            [work, work, *extra],
            flops=outs * (12 * n * n * naux * batch + 12 * n * n * n * batch),
            moved=4 * n * n * naux + 4 * size * (len(arrays) + outs),
        )(*arrays, high, low, plus, major, minor)

    mine = exchange(crossed.reshape(rows, local_cols // rows, local_rows), "row")
    first, double = operator(twice_body, [mine], gain, left, right, 2)
    first = exchange(first, "row").reshape(local_cols, local_rows)
    double = exchange(double, "row").reshape(local_cols, local_rows)

    theirs = exchange(turned.reshape(cols, local_rows // cols, local_cols), "col")
    base = operator(
        lambda n, *refs: once_body(n, time_step, time_step * time_step / 2.0, *refs),
        [theirs], -gain, right, left, 1,
    )
    first = call(
        turn_body, jax.ShapeDtypeStruct((local_rows, local_cols), f32), moved=8 * size
    )(first)
    first = exchange(first.reshape(cols, local_rows // cols, local_cols), "col")
    last = operator(
        added_body, [base, first], -gain, right, left, 1, [pltpu.VMEM(base.shape, f32)]
    )
    last = exchange(last, "col").reshape(local_rows, local_cols)

    return call(
        functools.partial(finish_body, n),
        jax.ShapeDtypeStruct(pairs.shape, f32),
        moved=16 * size,
    )(pairs, double, last)


def solution(mesh):
    body = functools.partial(shards, mesh.shape["row"], mesh.shape["col"])
    in_specs = (P("row", "col"), P(), P("row", "col", None), P())
    return jax.shard_map(
        body, mesh=mesh, in_specs=in_specs, out_specs=P("row", "col"), check_vma=False
    )
```

time: 1700 us -> 855 us (0.50)
  waiting for transfers between devices: 1050 us -> 260 us
  matrix products: 294 us -> 0 us
  blocking collectives: 0 us -> 264 us
  Pallas kernels: 0 us -> 260 us
  local copies, waits for them, and re-layouts: 267 us -> 22.8 us
  starting transfers between devices: 55.4 us -> 17.2 us
    all_to_all x8 -> x3, waiting for transfers between devices: 670 us -> 144 us  [exchange(): return lax.all_to_all(x, axis, split_axis=0, concat_axis=0, tiled=True)]
    dot_general x16 -> x0, matrix products: 294 us -> none  [the longest x2 58.9 us: derivative(): jnp.einsum('ijkm,ml->ijkl', field, one_body, precision=highest)]
    all_to_all x0 -> x3, blocking collectives: none -> 264 us  [exchange(): return lax.all_to_all(x, axis, split_axis=0, concat_axis=0, tiled=True)]
    pallas_call x0 -> x7, Pallas kernels: none -> 260 us  [the longest x3 166 us: operator(): call(functools.partial(body, n), [shape] * outs if outs > 1 else shape, [...]
    all_gather x6 -> x2, waiting for transfers between devices: 349 us -> 116 us  [the longest x1 73.4 us: shards(): whole = lax.all_gather(aux, 'row', axis=0, tiled=True)]
    all_to_all x14 -> x0, local copies, waits for them, and re-layouts: 130 us -> none  [the longest x4 39.8 us: derivative(): lax.all_to_all(applied, 'row', split_axis=0, concat_axis=1, tiled=True)]
    reshape x5 -> x0, local copies, waits for them, and re-layouts: 52.9 us -> none  [the longest x4 43.5 us: shards(): field = pairs.reshape(first_local, orbitals, third_local, orbitals)]
    all_to_all x8 -> x3, starting transfers between devices: 54.8 us -> 17.2 us  [exchange(): return lax.all_to_all(x, axis, split_axis=0, concat_axis=0, tiled=True)]
  transfers between devices with their start and end apart: 18 -> 5, of which waited for: 11 -> 5; matrix products, arithmetic and copies ran while one was open for 22% -> 2% of each run, Pallas kernels for 0% -> 17%
where the time goes in v1:
time: 855 us; the launch traced here: 839 us
  blocking collectives  264 us (31%)
  waiting for transfers between devices  260 us (30%)
  Pallas kernels  260 us (30%)
  local copies, waits for them, and re-layouts  22.8 us (3%)
  starting transfers between devices  17.2 us (2%)
  between operations  13.7 us (2%)
    all_to_all x3, blocking collectives, exchange(): return lax.all_to_all(x, axis, split_axis=0, concat_axis=0, tiled=True)  264 us
    pallas_call x3, Pallas kernels, operator(): call(functools.partial(body, n), [shape] * outs if outs > 1 else shape, [...  166 us
    all_to_all x3, waiting for transfers between devices, exchange(): return lax.all_to_all(x, axis, split_axis=0, concat_axis=0, tiled=True)  144 us
    all_gather x1, waiting for transfers between devices, shards(): whole = lax.all_gather(aux, 'row', axis=0, tiled=True)  73.4 us
    all_gather x1, waiting for transfers between devices, shards(): lax.all_gather(whole, 'col', axis=1, tiled=True).reshape(n * n, naux)  42.7 us
    pallas_call x1, Pallas kernels, shards(): call(functools.partial(finish_body, n), jax.ShapeDtypeStruct(pairs.shape,...  38.8 us
    pallas_call x1, Pallas kernels, shards(): call(functools.partial(regroup_body, n), [jax.ShapeDtypeStruct((local_col...  36.7 us
    all_to_all x3, starting transfers between devices, exchange(): return lax.all_to_all(x, axis, split_axis=0, concat_axis=0, tiled=True)  17.2 us
  transfers between devices with their start and end apart: 5, of which 5 were waited for; matrix products, arithmetic and copies ran while one was open for 2% of the time, Pallas kernels for 17%

profile of v1, /device:TPU:1, one launch (start us, length us, event | category | flops | bytes accessed | tf_op | source)
XLA Modules:
  0.0 839.5 jit_solution(16992676111111945750)
XLA Ops:
  6.5 0.0 all-gather.3.cloned.1.call-start
  6.5 0.7 all-gather.3.cloned.1.call-update
  7.3 0.0 all-gather.5.cloned.1.call-start
  7.3 73.4 %all-gather.3.cloned.1.call-done = f32[80,20,512]{2,1,0:T(8,128)} async-done(((f32[10,20,512]{2,1,0:T(8,128)}), f32[80,20,512]{2,1,0:T(8,128)}) %all-gather.3.cloned.1.call-update) | async-done | bytes 3276816 | tf_op jit(solution)/shard_map/all_gather | solution.py:191
  80.7 5.7 copy.6
  86.4 0.0 all-gather.5.cloned.1.call-update
  86.4 36.7 %shard_map.46 = (f32[1600,800]{1,0:T(8,128)}, f32[800,1600]{1,0:T(8,128)}) custom-call(f32[800,1600]{1,0:T(8,128)} %x_ref.3), custom_call_target="tpu_custom_call" | custom-call | bytes 15360000 | tf_op jit(solution)/shard_map/pallas_call | solution.py:212
  123.1 0.0 copy-start
  123.1 4.8 all-to-all-start
  128.0 0.0 copy-done
  128.0 0.1 copy.8
  128.1 0.7 pad_maximum_fusion
  128.8 42.7 %all-gather.5.cloned.1.call-done = f32[80,80,512]{2,0,1:T(8,128)} async-done(((f32[80,20,512]{2,0,1:T(8,128)}), f32[80,80,512]{2,0,1:T(8,128)}) %all-gather.5.cloned.1.call-update) | async-done | bytes 13107216 | tf_op jit(solution)/shard_map/all_gather | solution.py:192
  171.6 17.1 %copy.7 = f32[80,80,512]{2,1,0:T(8,128)} copy(f32[80,80,512]{2,0,1:T(8,128)} %all-gather.5.cloned.1.call-done) | data formatting | bytes 26214400 | tf_op jit(solution)/shard_map/all_gather | solution.py:192
  188.6 11.8 %shard_map.47 = (bf16[6400,512]{1,0:T(8,128)(2,1)}, bf16[6400,512]{1,0:T(8,128)(2,1)}) custom-call(f32[6400,512]{1,0:T(8,128)} %bitcast.12), custom_call_target="tpu_custom_call" | custom-call | flops 6553600 | bytes 26214400 | tf_op jit(solution)/shard_map/pallas_call | solution.py:196
  200.4 52.0 %all-to-all-done.x_ref = f32[8,200,800]{2,1,0:T(8,128)} async-done(((f32[8,200,800]{2,1,0:T(8,128)}), f32[8,200,800]{2,1,0:T(8,128)}, u32[]{:S(2)}, u32[]{:S(2)}) %all-to-all-start) | async-done | bytes 5120032 | tf_op jit(solution)/shard_map/all_to_all | solution.py:182
  252.4 79.8 %shard_map.48 = (f32[8,200,800]{2,1,0:T(8,128)}, f32[8,200,800]{2,1,0:T(8,128)}) custom-call(f32[8,200,800]{2,1,0:T(8,128)} %all-to-all-done.x_ref, bf16[6400,512]{1,0:T(8,128)(2,1)} %get-tuple-element.12.high_ref.refs_1_.refs_0_, bf16[6400,512]{1,0:T(8,128)(2,1)} %get-tuple-element.13.low_ref.refs_2_.refs_1_, f32[1,512]{1,0:T(1,128)} %bitcast.18, ...), custom_call_target="tpu_custom_call" | custom-call | flops 18186240000 | bytes 28467200 | tf_op jit(solution)/shard_map/pallas_call | solution.py:225
  332.2 130.3 %all_to_all.30 = f32[8,200,800]{2,1,0:T(8,128)} all-to-all(f32[8,200,800]{2,1,0:T(8,128)} %get-tuple-element.16), channel_id=1, replica_groups=mesh['row'=8,'col'=4] {'row'}, dimensions={0} | all-to-all | bytes 10240000 | tf_op jit(solution)/shard_map/all_to_all | solution.py:182
  462.5 7.5 all-to-all-start.2
  470.0 6.6 shard_map.50
  476.6 53.0 %all-to-all-done.2.refs_0_ = f32[4,200,1600]{2,1,0:T(8,128)} async-done(((f32[4,200,1600]{2,1,0:T(8,128)}), f32[4,200,1600]{2,1,0:T(8,128)}, u32[]{:S(2)}, u32[]{:S(2)}) %all-to-all-start.2) | async-done | bytes 5120032 | tf_op jit(solution)/shard_map/all_to_all | solution.py:182
  529.6 66.5 %all_to_all.31.z_ref = f32[4,200,1600]{2,1,0:T(8,128)} all-to-all(f32[4,200,1600]{2,1,0:T(8,128)} %bitcast.15), channel_id=1, replica_groups=mesh['row'=8,'col'=4] {'col'}, dimensions={0} | all-to-all | bytes 10240000 | tf_op jit(solution)/shard_map/all_to_all | solution.py:182
  596.0 0.0 copy-start.1
  596.0 4.8 all-to-all-start.1
  600.9 0.0 copy-done.1
  600.9 0.6 neg.14
  601.5 42.2 %shard_map.49.x_ref = f32[4,200,1600]{2,1,0:T(8,128)} custom-call(f32[4,200,1600]{2,1,0:T(8,128)} %all-to-all-done.2.refs_0_, bf16[6400,512]{1,0:T(8,128)(2,1)} %get-tuple-element.12.high_ref.refs_1_.refs_0_, bf16[6400,512]{1,0:T(8,128)(2,1)} %get-tuple-element.13.low_ref.refs_2_.refs_1_, f32[1,512]{1,0:T(1,128)} %bitcast.19, ...), custom_call_target="tpu_custom_call" | custom-call | flops 9093120000 | bytes 23347200 | tf_op jit(solution)/shard_map/pallas_call | solution.py:225
  643.7 44.1 %shard_map.51 = f32[4,200,1600]{2,1,0:T(8,128)} custom-call(f32[4,200,1600]{2,1,0:T(8,128)} %shard_map.49.x_ref, f32[4,200,1600]{2,1,0:T(8,128)} %all_to_all.31.z_ref, bf16[6400,512]{1,0:T(8,128)(2,1)} %get-tuple-element.12.high_ref.refs_1_.refs_0_, bf16[6400,512]{1,0:T(8,128)(2,1)} %get-tuple-element.13.low_ref.refs_2_.refs_1_, f32[1,512]{1,0:T(1,128)} %bitcast.20, ...), custom_call_target="tpu_custom_call" | custom-call | flops 9093120000 | bytes 28467200 | tf_op jit(solution)/shard_map/pallas_call | solution.py:225
  687.8 38.6 %all-to-all-done.1 = f32[8,200,800]{2,1,0:T(8,128)} async-done(((f32[8,200,800]{2,1,0:T(8,128)}), f32[8,200,800]{2,1,0:T(8,128)}, u32[]{:S(2)}, u32[]{:S(2)}) %all-to-all-start.1) | async-done | bytes 5120032 | tf_op jit(solution)/shard_map/all_to_all | solution.py:182
  726.3 67.3 %all_to_all.32 = f32[4,200,1600]{2,1,0:T(8,128)} all-to-all(f32[4,200,1600]{2,1,0:T(8,128)} %shard_map.51), channel_id=1, replica_groups=mesh['row'=8,'col'=4] {'col'}, dimensions={0} | all-to-all | bytes 10240000 | tf_op jit(solution)/shard_map/all_to_all | solution.py:182
  793.6 38.8 %shard_map.52 = f32[800,1600]{1,0:T(8,128)} custom-call(f32[800,1600]{1,0:T(8,128)} %x_ref.3, f32[1600,800]{1,0:T(8,128)} %bitcast.4.crossed_ref, f32[800,1600]{1,0:T(8,128)} %bitcast.14), custom_call_target="tpu_custom_call" | custom-call | bytes 20480000 | tf_op jit(solution)/shard_map/pallas_call | solution.py:252
  (2 shorter events, 0.0 us)
Async XLA Ops:
  6.5 74.1 %all-gather.3.cloned.1.call-start = ((), (), s32[]{:S(2)}) async-start(), calls=%async_computation.6 | async-start | bytes 4423680 | tf_op jit(solution)/shard_map/all_gather | solution.py:191
  7.3 164.3 %all-gather.5.cloned.1.call-start = ((), (), s32[]{:S(2)}) async-start(), calls=%async_computation.7 | async-start | bytes 16384000 | tf_op jit(solution)/shard_map/all_gather | solution.py:192
  123.1 4.8 copy-start
  123.1 129.3 %all-to-all-start = ((f32[8,200,800]{2,1,0:T(8,128)}), f32[8,200,800]{2,1,0:T(8,128)}, u32[]{:S(2)}, u32[]{:S(2)}) async-start(f32[8,200,800]{2,1,0:T(8,128)} %bitcast.16), calls=%async_computation | async-start | bytes 11468800 | tf_op jit(solution)/shard_map/all_to_all | solution.py:182
  462.5 67.0 %all-to-all-start.2 = ((f32[4,200,1600]{2,1,0:T(8,128)}), f32[4,200,1600]{2,1,0:T(8,128)}, u32[]{:S(2)}, u32[]{:S(2)}) async-start(f32[4,200,1600]{2,1,0:T(8,128)} %bitcast.17), calls=%async_computation.2 | async-start | bytes 10649600 | tf_op jit(solution)/shard_map/all_to_all | solution.py:182
  596.0 4.8 copy-start.1
  596.0 130.3 %all-to-all-start.1 = ((f32[8,200,800]{2,1,0:T(8,128)}), f32[8,200,800]{2,1,0:T(8,128)}, u32[]{:S(2)}, u32[]{:S(2)}) async-start(f32[8,200,800]{2,1,0:T(8,128)} %get-tuple-element.14), calls=%async_computation.1 | async-start | bytes 11468800 | tf_op jit(solution)/shard_map/all_to_all | solution.py:182
Sparse Core Ops, SparseCore 0:
  9.5 71.0 all-gather.2
  86.5 85.0 all-gather.4
